TPU v7x, 128 devices: a whole 4x4x4 slice. The times are simulated.
128 devices in a mesh: dp: 4 (over y), seq: 16 (over z, x_lo, core), wshard: 2 (over x_hi).
Axes of the slice: x: 4 (x_hi: 2, x_lo: 2; x = x_hi * 2 + x_lo), y: 4, z: 4, core: 2. Of those that a mesh axis runs over, the one named last changes fastest.
Arguments:
- tokens: bfloat16 [8, 4096, 1024], P('dp', ('seq', 'wshard')), may hold values from -6 to 6
- segments: int32 [8, 4096], P('dp', ('seq', 'wshard')), may hold values from 0 to 20, as said below
- valid_flags: int32 [8, 4096], P('dp', ('seq', 'wshard')), may hold values from 0 to 1, as said below
- teacher: bfloat16 [8, 4096, 1024], P('dp', ('seq', 'wshard')), may hold values from -6 to 6
- w_qkv: bfloat16 [1024, 3072], P(('dp', 'wshard')), may hold values from -0.1875 to 0.1875
- b_query: bfloat16 [1024], P(('dp', 'wshard')), may hold values from -3 to 3
- b_value: bfloat16 [1024], P(('dp', 'wshard')), may hold values from -3 to 3
- w_out: bfloat16 [1024, 1024], P(('dp', 'wshard')), may hold values from -1.5 to 1.5
- b_out: bfloat16 [1024], P(('dp', 'wshard')), may hold values from -3 to 3
- ln1_gain: bfloat16 [1024], P(('dp', 'wshard')), may hold values from 0.099609375 to 1.8984375
- ln1_bias: bfloat16 [1024], P(('dp', 'wshard')), may hold values from -3 to 3
- w_up: bfloat16 [1024, 4096], P(('dp', 'wshard')), may hold values from -0.1875 to 0.1875
- b_up: bfloat16 [4096], P(('dp', 'wshard')), may hold values from -3 to 3
- w_down: bfloat16 [4096, 1024], P(('dp', 'wshard')), may hold values from -0.09375 to 0.09375
- b_down: bfloat16 [1024], P(('dp', 'wshard')), may hold values from -3 to 3
- ln2_gain: bfloat16 [1024], P(('dp', 'wshard')), may hold values from 0.099609375 to 1.8984375
- ln2_bias: bfloat16 [1024], P(('dp', 'wshard')), may hold values from -3 to 3
Outputs:
- states: bfloat16 [8, 4096, 1024], P('dp', ('seq', 'wshard'))
- mean_loss: float32 [], replicated
- grad_tokens: float32 [8, 4096, 1024], P('dp', ('seq', 'wshard'))
- grad_w_qkv: float32 [1024, 3072], P(('dp', 'wshard'))
- grad_b_query: float32 [1024], P(('dp', 'wshard'))
- grad_b_value: float32 [1024], P(('dp', 'wshard'))
- grad_w_out: float32 [1024, 1024], P(('dp', 'wshard'))
- grad_b_out: float32 [1024], P(('dp', 'wshard'))
- grad_ln1_gain: float32 [1024], P(('dp', 'wshard'))
- grad_ln1_bias: float32 [1024], P(('dp', 'wshard'))
- grad_w_up: float32 [1024, 4096], P(('dp', 'wshard'))
- grad_b_up: float32 [4096], P(('dp', 'wshard'))
- grad_w_down: float32 [4096, 1024], P(('dp', 'wshard'))
- grad_b_down: float32 [1024], P(('dp', 'wshard'))
- grad_ln2_gain: float32 [1024], P(('dp', 'wshard'))
- grad_ln2_bias: float32 [1024], P(('dp', 'wshard'))
Inputs may be any that keep to these rules, and one draw needn't show every extreme that they name: `segments`: segment numbers start at 0 in each sequence and never fall along it; a document has 204 to 2048 tokens except the last one of a sequence, which may be cut. In every run of 2 sequences held by one index of dp, one sequence is a single document. In some sequence every document but the last has exactly 204 tokens. `valid_flags`: the first token of every sequence is valid.
All inputs are finite; a program needn't handle non-finite values.
Results may differ from a plain program's by a relative error of at most 0.017.
Values may be sent and summed in bfloat16 or wider, within the bound.
A program may use at most 128 MiB of HBM per device.

v0:
```python
import functools

import jax
import jax.numpy as jnp
from jax import lax
from jax.experimental import pallas as pl
from jax.experimental.pallas import tpu as pltpu
from jax.sharding import PartitionSpec as P

D = 1024
H = 16
HD = 64
FF = 4096
L = 4096
EPS = 1e-06
F32 = jnp.float32
BF = jnp.bfloat16
MASKED = 1000000000.0
VMEM_CAP = 60 * 1024 * 1024
MESH = pl.DeviceIdType.MESH
ANY = pl.BlockSpec(memory_space=pl.ANY)
TB = 128
NB = L // TB


def dot(first, second, dims=((1,), (0,))):
    return lax.dot_general(first, second, (dims, ((), ())), preferred_element_type=F32)


def three_pieces(row):
    high = row.astype(BF)
    rest = row - high.astype(F32)
    middle = rest.astype(BF)
    lowest = (rest - middle.astype(F32)).astype(BF)
    return jnp.concatenate([high, middle, lowest], axis=0)


def place():
    at = lax.axis_index("seq")
    return (lax.axis_index("wshard") * 2 + (at // 2) % 2, lax.axis_index("dp"), at // 4, at % 2)


def device_at(x, y, z, core):
    return (y, (z * 2 + x % 2) * 2 + core, x // 2)


def along(axis, shift):
    x, y, z, core = place()
    if axis == "x":
        return device_at((x + shift) % 4, y, z, core)
    if axis == "y":
        return device_at(x, (y + shift) % 4, z, core)
    return device_at(x, y, (z + shift) % 4, core)


def sibling():
    x, y, z, core = place()
    return device_at(x, y, z, 1 - core)


def greet(partners):
    barrier = pltpu.get_barrier_semaphore()
    for partner in partners:
        pl.semaphore_signal(barrier, inc=1, device_id=partner, device_id_type=MESH)
    pl.semaphore_wait(barrier, len(partners))


def remote(src, dst, send_sem, recv_sem, target):
    return pltpu.make_async_remote_copy(
        src_ref=src, dst_ref=dst, send_sem=send_sem, recv_sem=recv_sem, device_id=target, device_id_type=MESH
    )


ORDERS = ("yzx", "zxy", "xyz")
PIECE = (64, 32, 48)
FIRST = (0, 512, 768)


def ring_partners():
    return [along(axis, shift) for axis in "xyz" for shift in (1, 2, 3)] + [sibling()]


def reduce_scratch():
    a, b, c = PIECE
    return [
        pltpu.VMEM((4, 2, 8 * a, 512), BF),
        pltpu.VMEM((4, 4, 2, 2 * b, 512), BF),
        pltpu.VMEM((4, 4, 4 * c, 512), BF),
        pltpu.VMEM((4, 2, 2 * a, 512), BF),
        pltpu.VMEM((4, 4, b, 512), BF),
        pltpu.VMEM((4, 4 * c, 512), BF),
        pltpu.VMEM((4, a, 512), BF),
        pltpu.VMEM((4, b, 512), BF),
        pltpu.VMEM((4, c, 512), BF),
        pltpu.SemaphoreType.DMA((3, 3, 3)),
        pltpu.SemaphoreType.DMA((3, 3, 3)),
        pltpu.SemaphoreType.DMA((3,)),
        pltpu.VMEM((2, 8 * a, 512), BF),
        pltpu.SemaphoreType.DMA((6,)),
        pltpu.SemaphoreType.DMA((6,)),
        pltpu.SemaphoreType.DMA((2,)),
    ]


def aligned(value, unit):
    return pl.multiple_of(value, unit)


def reduce_piece(stage, part, refs, at):
    g_ref = refs[0]
    half, low, n = at // 2, at % 2, PIECE[part]
    if stage == 0:
        first = FIRST[part]
        if part == 0:
            return g_ref.at[at, :, pl.ds(first, 8 * n), :]
        if part == 1:
            return g_ref.at[:, :, pl.ds(aligned(first + at * 2 * n, 16), 2 * n), :]
        return g_ref.at[:, half, pl.ds(aligned(first + low * 4 * n, 16), 4 * n), :]
    held = refs[1 + 3 * (stage - 1) + part]
    if stage == 1:
        if part == 0:
            return held.at[0, :, pl.ds(aligned(at * 2 * n, 16), 2 * n), :]
        if part == 1:
            return held.at[0, :, half, pl.ds(aligned(low * n, 16), n), :]
        return held.at[0, at]
    if part == 0:
        return held.at[0, half, pl.ds(aligned(low * n, 16), n), :]
    if part == 1:
        return held.at[0, at]
    return held.at[0, pl.ds(aligned(at * n, 16), n), :]


def ring_at(axis):
    x, y, z, _ = place()
    return {"x": x, "y": y, "z": z}[axis]


def reduce_copies(stage, part, refs):
    send, recv = refs[10], refs[11]
    axis = ORDERS[part][stage]
    return [
        remote(
            reduce_piece(stage, part, refs, (ring_at(axis) + shift) % 4),
            refs[1 + 3 * stage + part].at[shift],
            send.at[stage, part, shift - 1],
            recv.at[stage, part, shift - 1],
            along(axis, shift),
        )
        for shift in (1, 3, 2)
    ]


def reduce_own(part, refs):
    return pltpu.make_async_copy(
        reduce_piece(0, part, refs, ring_at(ORDERS[part][0])), refs[1 + part].at[0], refs[12].at[part]
    )


def reduce_start(part, refs):
    start_all(first_copies(refs)[:4] + first_loads(refs) if part == 0 else reduce_copies(0, part, refs))
    reduce_own(part, refs).start()


def first_copies(refs):
    g_ref, a1, relay, send, recv = refs[0], refs[1], refs[13], refs[14], refs[15]
    _, y, _, _ = place()
    rows = pl.ds(0, 8 * PIECE[0])
    up, down, far = (y + 1) % 4, (y + 3) % 4, (y + 2) % 4
    moves = [
        (g_ref.at[far, 0, rows], a1.at[2, 0], 1),
        (g_ref.at[far, 1, rows], a1.at[2, 1], 3),
        (g_ref.at[up, 1, rows], a1.at[1, 1], 1),
        (g_ref.at[down, 0, rows], a1.at[3, 0], 3),
        (relay.at[0], a1.at[1, 0], 1),
        (relay.at[1], a1.at[3, 1], 3),
    ]
    return [remote(src, dst, send.at[k], recv.at[k], along("y", d)) for k, (src, dst, d) in enumerate(moves)]


def first_loads(refs):
    g_ref, relay, local = refs[0], refs[13], refs[16]
    _, y, _, _ = place()
    rows = pl.ds(0, 8 * PIECE[0])
    return [
        pltpu.make_async_copy(g_ref.at[(y + 1) % 4, 0, rows], relay.at[0], local.at[0]),
        pltpu.make_async_copy(g_ref.at[(y + 3) % 4, 1, rows], relay.at[1], local.at[1]),
    ]


def first_relay(refs):
    a1, relay = refs[1], refs[13]
    copies = first_copies(refs)
    wait_all(first_loads(refs))
    for copy in copies[:2]:
        copy.wait_recv()

    @pl.loop(0, 16)
    def _(i):
        rows = pl.ds(aligned((i % 8) * PIECE[0], 16), PIECE[0])
        half = i // 8
        relay[half, rows, :] = (relay[half, rows, :].astype(F32) + a1[2, half, rows, :].astype(F32)).astype(BF)

    start_all(copies[4:])


def first_end(refs):
    copies = first_copies(refs)
    for copy in copies[:2]:
        copy.wait_send()
    wait_all(copies[2:])


def add_four(values):
    total = values[0].astype(F32) + values[1].astype(F32)
    return (total + values[2].astype(F32) + values[3].astype(F32)).astype(BF)


def reduce_step(stage, part, refs):
    a1, b1, c1, a2, b2, c2, a3, b3, c3 = refs[1:10]
    if stage == 0 and part == 0:
        first_end(refs)
    else:
        wait_all(reduce_copies(stage, part, refs))
    x, y, z, _ = place()
    n = PIECE[part]
    rest = (1, 2, 3)
    if stage == 0:
        reduce_own(part, refs).wait()

        @pl.loop(0, 16)
        def _(i):
            if part == 0:
                rows = pl.ds(aligned((i % 8) * n, 16), n)
                total = a1[0, i // 8, rows, :].astype(F32) + a1[1, i // 8, rows, :].astype(F32)
                a1[0, i // 8, rows, :] = (total + a1[3, i // 8, rows, :].astype(F32)).astype(BF)
            elif part == 1:
                rows = pl.ds(aligned((i % 2) * n, 16), n)
                b1[0, i // 4, (i // 2) % 2, rows, :] = add_four([b1[s, i // 4, (i // 2) % 2, rows, :] for s in range(4)])
            else:
                rows = pl.ds(aligned((i % 4) * n, 16), n)
                c1[0, i // 4, rows, :] = add_four([c1[s, i // 4, rows, :] for s in range(4)])

    elif stage == 1:

        @pl.loop(0, 4)
        def _(i):
            if part == 0:
                rows = pl.ds(aligned((i % 2) * n, 16), n)
                own = a1[0, i // 2, pl.ds(aligned(z * 2 * n + (i % 2) * n, 16), n), :]
                a2[0, i // 2, rows, :] = add_four([own] + [a2[s, i // 2, rows, :] for s in rest])
            elif part == 1:
                own = b1[0, i, x // 2, pl.ds(aligned((x % 2) * n, 16), n), :]
                b2[0, i] = add_four([own] + [b2[s, i] for s in rest])
            else:
                rows = pl.ds(aligned(i * n, 16), n)
                own = c1[0, y, rows, :]
                c2[0, rows, :] = add_four([own] + [c2[s, rows, :] for s in rest])

    elif part == 0:
        own = a2[0, x // 2, pl.ds(aligned((x % 2) * n, 16), n), :]
        a3[0] = add_four([own] + [a3[s] for s in rest])
    elif part == 1:
        b3[0] = add_four([b2[0, y]] + [b3[s] for s in rest])
    else:
        own = c2[0, pl.ds(aligned(z * n, 16), n), :]
        c3[0] = add_four([own] + [c3[s] for s in rest])
    if stage < 2:
        start_all(reduce_copies(stage + 1, part, refs))


def shard_rows(o_ref, part, x_low, z, core):
    sub = x_low * 4 + z if part == 2 else z * 2 + x_low
    return o_ref.at[core, pl.ds(aligned(FIRST[part] + sub * PIECE[part], 16), PIECE[part]), :]


def spread_steps(part, mine, sems, o_ref):
    local, send, recv = sems
    x, y, z, core = place()
    low = x % 2
    pair = device_at(x // 2 * 2 + 1 - low, y, z, core)
    spot = shard_rows(o_ref, part, low, z, core)
    own = pltpu.make_async_copy(mine, spot, local.at[part])
    first = remote(mine, spot, send.at[part, 0], recv.at[part, 0], pair)
    second = [remote(mine, spot, send.at[part, d], recv.at[part, d], along("z", d)) for d in (1, 3, 2)]
    spot = shard_rows(o_ref, part, 1 - low, z, core)
    third = [remote(spot, spot, send.at[part, 3 + d], recv.at[part, 3 + d], along("z", d)) for d in (1, 3, 2)]

    def begin():
        start_all([own, first] + second)

    def middle():
        first.wait()
        start_all(third)

    def end():
        wait_all([own] + second + third)

    return begin, middle, end


def swap_partner(shift):
    mine = lax.axis_index("seq") * 2 + lax.axis_index("wshard")
    other = (mine + shift) % NB
    return other, (lax.axis_index("dp"), other // 2, other % 2)


def swap_greet():
    barrier = pltpu.get_barrier_semaphore()

    @pl.loop(1, NB)
    def _(shift):
        pl.semaphore_signal(barrier, inc=1, device_id=swap_partner(shift)[1], device_id_type=MESH)

    pl.semaphore_wait(barrier, NB - 1)


def swap_copies(piece_for, landing_from, sems):
    mine = lax.axis_index("seq") * 2 + lax.axis_index("wshard")
    send, recv, local = sems

    def copy(shift):
        other, device = swap_partner(shift)
        return remote(piece_for(other), landing_from(mine), send.at[shift], recv.at[shift], device)

    own = pltpu.make_async_copy(piece_for(mine), landing_from(mine), local)

    def start():
        @pl.loop(1, NB)
        def _(shift):
            copy(shift).start()

        own.start()

    def wait():
        @pl.loop(1, NB)
        def _(shift):
            copy(shift).wait()

        own.wait()

    return start, wait


def swap_sems():
    return [pltpu.SemaphoreType.DMA((NB,)), pltpu.SemaphoreType.DMA((NB,)), pltpu.SemaphoreType.DMA]


def block_of(ref, b):
    return ref.at[b]


def head_tile(ref, b):
    return ref.at[pl.ds(aligned((b // 2) * HD, HD), HD), pl.ds(aligned((b % 2) * TB, TB), TB)]


def head_tile3(ref, b):
    return ref.at[:, pl.ds(aligned((b // 2) * HD, HD), HD), pl.ds(aligned((b % 2) * TB, TB), TB)]


HALVES = ((128, 2048), (256, 1024))


class Transfers:
    def __init__(self, send, recv):
        self.send, self.recv, self.used = send, recv, 0

    def copy(self, src, dst, target):
        made = remote(src, dst, self.send.at[self.used], self.recv.at[self.used], target)
        self.used += 1
        return made


def start_all(copies):
    for copy in copies:
        copy.start()


def wait_all(copies):
    for copy in copies:
        copy.wait()


def unit_rows(matrix, unit, count=1):
    rows = HALVES[matrix][0] // 4
    return pl.ds(unit * rows, count * rows)


def columns_part(matrix, at, parts):
    width = HALVES[matrix][1] // parts
    return pl.ds(aligned(at * width, 128), width)


def half_rows(core, rows=64):
    return pl.ds(aligned(core * rows, rows), rows)


def shard_greet():
    x, y, z, core = place()
    return [device_at(x, (y + d) % 4, z, core) for d in (1, 2, 3)] + [
        device_at(3 - x, (y + d) % 4, z, core) for d in range(4)
    ]


def greet_signal(others):
    barrier = pltpu.get_barrier_semaphore()

    @pl.loop(1, NB)
    def _(shift):
        pl.semaphore_signal(barrier, inc=1, device_id=swap_partner(shift)[1], device_id_type=MESH)

    for other in others:
        pl.semaphore_signal(barrier, inc=1, device_id=other, device_id_type=MESH)


def greet_wait(others):
    pl.semaphore_wait(pltpu.get_barrier_semaphore(), NB - 1 + len(others))


FRONT_COPIES = 144


def front_kernel(
    tokens, segments, flags, vectors, b_up, w_out, w_up, w_down, w_qkv,
    x_seq, meta_out, smalls_out, out_all, up_all, down_all, qkv_all, qat_ref, ka_ref, va_ref, kt_ref, q_ref,
    context, wide_ref, lse_ref,
    vat_ref, blocks, x_buf, tok_buf, out_buf, up_buf, down_buf, qkv_buf, meta, heads, smalls, meta_all, heads_all, smalls_all, w_ref, b_ref,
    send, recv, local, meta_send, meta_recv, meta_local, back_send, back_recv, back_local,
):
    x, y, z, core = place()
    hi, lo = x // 2, x % 2
    mine, across = y * 2 + hi, y * 2 + 1 - hi
    wrap, pair, other_core = device_at(3 - x, y, z, core), device_at(hi * 2 + 1 - lo, y, z, core), sibling()
    shards, wholes = (up_buf.at[core], down_buf), (up_all, down_all)
    rows_out = half_rows(core)
    greet_signal(shard_greet())
    load_tokens = pltpu.make_async_copy(tokens, tok_buf, local.at[0])
    load_qkv = pltpu.make_async_copy(w_qkv, qkv_buf, local.at[11])
    loads = [
        pltpu.make_async_copy(w_out, out_buf, local.at[9]),
        pltpu.make_async_copy(w_down.at[half_rows(core, 256)], down_buf, local.at[10]),
    ]
    for j in range(8):
        piece = w_up.at[:, pl.ds(aligned(j * 512 + core * 256, 256), 256)]
        loads.append(pltpu.make_async_copy(piece, up_buf.at[core, :, pl.ds(j * 256, 256)], local.at[1 + j]))
    start_all([load_tokens, load_qkv] + loads)
    meta[...] = jnp.zeros_like(meta)
    for s in range(2):
        meta[s, 0:1, :] = segments[s : s + 1, :]
        meta[s, 1:2, :] = flags[s : s + 1, :]
    smalls[...] = jnp.zeros_like(smalls)
    smalls[0:8, :] = vectors[...]
    smalls[8:12, :] = b_up[...]
    greet_wait(shard_greet())
    load_tokens.wait()
    net = Transfers(send, recv)
    first, second = pl.ds(0, 64), pl.ds(64, 64)

    def block(at, low, w, rows=slice(None)):
        return x_buf.at[at, low, core, w, rows]

    own = tok_buf.at[hi]
    swap = net.copy(tok_buf.at[1 - hi], block(z, lo, hi), wrap)
    own_z = [net.copy(own, block(z, lo, hi), along("z", d)) for d in (1, 3, 2)]
    own_pair = [net.copy(own.at[rows], block(z, lo, hi, rows), pair) for rows in (first, second)]
    start_all([swap, own_pair[0]] + own_z)
    x_buf[z, lo, core, hi] = tok_buf[hi]
    load_qkv.wait()
    for p in range(3):
        for k, pair_at in ((0, z * 2 + lo), (1, z * 2 + 1 - lo)):
            heads[k, :, 128 * p : 128 * (p + 1)] = qkv_buf[:, pl.ds(aligned(p * D + pair_at * 128, 128), 128)]
    cross_first = [
        net.copy(heads.at[1], heads_all.at[mine], wrap),
        net.copy(smalls, smalls_all.at[mine], wrap),
    ]
    start_all(cross_first)

    def small_y(shard, heads_source, smalls_source):
        copies = []
        for d in (1, 3, 2):
            copies.append(net.copy(heads_source, heads_all.at[shard], along("y", d)))
            copies.append(net.copy(smalls_source, smalls_all.at[shard], along("y", d)))
        return copies

    own_small = small_y(mine, heads.at[0], smalls)
    start_all(own_small)
    heads_all[mine] = heads[0]
    smalls_all[mine] = smalls[...]
    meta_start, meta_wait = swap_copies(
        lambda b: meta.at[b % 2], lambda b: meta_all.at[b], (meta_send, meta_recv, meta_local)
    )
    meta_start()
    wait_all(loads)
    keep = [
        pltpu.make_async_copy(out_buf.at[rows_out], out_all.at[mine, rows_out], local.at[9]),
        pltpu.make_async_copy(qkv_buf, qkv_all.at[mine], local.at[11]),
    ]
    for m in range(2):
        parts = [
            (unit_rows(m, 0), columns_part(m, z, 4)),
            (unit_rows(m, 3), columns_part(m, lo, 2)),
            (unit_rows(m, 1, 2), slice(None)),
        ]
        for k, (rows, columns) in enumerate(parts):
            piece = wholes[m].at[mine, rows, columns]
            keep.append(pltpu.make_async_copy(shards[m].at[rows, columns], piece, local.at[1 + 3 * m + k]))
    start_all(keep)

    def along_y(shard, source, out_source, up_unit):
        copies = []
        for d in (1, 3, 2):
            there = along("y", d)
            copies.append(net.copy(out_source.at[rows_out], out_all.at[shard, rows_out], there))
            for m in range(2):
                parts = [(0, columns_part(m, z, 4)), (3, columns_part(m, lo, 2))]
                if up_unit:
                    parts.append((1, slice(None)))
                for unit, columns in parts:
                    rows = unit_rows(m, unit, 2 if m == 1 and unit == 1 else 1)
                    copies.append(net.copy(source(m).at[rows, columns], wholes[m].at[shard, rows, columns], there))
        return copies

    own_y = along_y(mine, lambda m: shards[m], out_buf, True)
    start_all(own_y)
    swap.wait_recv()
    came = block(z, 1 - lo, 1 - hi)
    came_pair = [
        net.copy(block(z, 1 - lo, 1 - hi, rows), block(z, 1 - lo, 1 - hi, rows), pair) for rows in (first, second)
    ]
    came_z = [net.copy(came, came, along("z", d)) for d in (1, 3, 2)]
    start_all([came_pair[0]] + came_z + [own_pair[1], came_pair[1]])
    cross_early, cross_late = [net.copy(out_buf.at[rows_out], out_all.at[mine, rows_out], wrap)], []
    for m in range(2):
        for unit, columns in ((0, columns_part(m, z, 4)), (3, columns_part(m, 1 - lo, 2))):
            rows = unit_rows(m, unit)
            cross_early.append(net.copy(shards[m].at[rows, columns], wholes[m].at[mine, rows, columns], wrap))
    rows = unit_rows(0, 1, 2)
    cross_late.append(net.copy(shards[0].at[rows], up_all.at[mine, rows], wrap))
    rows = half_rows(core)
    cross_late.append(net.copy(qkv_buf.at[rows], qkv_all.at[mine, rows], wrap))
    start_all(cross_early)
    pair_late = []

    def forward(got, d, low, w):
        got.wait_recv()
        piece = block((z + 4 - d) % 4, low, w, second)
        pair_late.append(net.copy(piece, piece, pair))
        pair_late[-1].start()

    for i, d in enumerate((1, 3, 2)):
        forward(own_z[i], d, lo, hi)
    for copy in cross_first:
        copy.wait_recv()
    across_small = small_y(across, heads_all.at[across], smalls_all.at[across])
    start_all(across_small)
    half_z = []

    def halves(got, low, w):
        got.wait_recv()
        piece = block(z, low, w, first)
        copies = [net.copy(piece, piece, along("z", d)) for d in (1, 3, 2)]
        start_all(copies)
        half_z.extend(copies)

    halves(own_pair[0], 1 - lo, hi)
    for copy in cross_early:
        copy.wait_recv()
    across_y = along_y(across, lambda m: wholes[m].at[across], out_all.at[across], False)
    start_all(across_y + cross_late)
    for i, d in enumerate((1, 3, 2)):
        forward(came_z[i], d, 1 - lo, 1 - hi)
    halves(came_pair[0], lo, 1 - hi)
    share, rest = [], []
    for low, w in ((lo, hi), (1 - lo, 1 - hi)):
        piece = x_buf.at[:, low, core, w]
        share.append(net.copy(piece, piece, other_core))
    start_all(share)

    for copy in own_small + across_small:
        copy.wait_recv()
    meta_wait()
    at_first = core == 0
    both = heads_all[...].reshape(D, 384)
    parts = [jnp.where(at_first, both[:, 128 * p : 128 * p + HD], both[:, 128 * p + HD : 128 * (p + 1)]) for p in range(3)]
    w_ref[...] = jnp.concatenate(parts, axis=1)
    biases = smalls_all[lax.axis_index("seq") // 2]
    bias = [jnp.where(at_first, biases[k : k + 1, :HD], biases[k : k + 1, HD:]) for k in range(2)]
    b_ref[...] = jnp.broadcast_to(jnp.concatenate([bias[0], jnp.zeros((1, HD), F32), bias[1]], axis=1), (8, 3 * HD))

    def project(low, at_core, w):
        @pl.loop(0, 4)
        def _(at):
            b = at * 8 + low * 4 + at_core * 2 + w
            rows = pl.ds(aligned(b * TB, TB), TB)
            side = dot(x_buf[at, low, at_core, w], w_ref[...]) + b_ref[:1, :]
            q8 = side[:, :HD].astype(BF).astype(F32) * 0.125
            hot = jnp.where(lax.broadcasted_iota(jnp.int32, (32, TB), 0) == meta_all[b, 0:1, :], 1.0, 0.0)
            lane = lax.broadcasted_iota(jnp.int32, (TB, HD), 1)
            ones3 = jnp.where(lane < 3, 1.0, 0.0)
            apart = (hot.T - 1.0) * MASKED
            key = side[:, HD : 2 * HD]
            value = side[:, 2 * HD :]
            q_ref[rows, :] = q8.astype(BF)
            ka_ref[rows, :] = jnp.concatenate([key, apart, ones3[:, :32]], axis=1).astype(BF)
            va_ref[rows, :] = jnp.concatenate([value, ones3], axis=1).astype(BF)
            qat_ref[:, rows] = jnp.concatenate([q8.T, hot, jnp.zeros((32, TB), F32)], axis=0).astype(BF)
            kt_ref[:, rows] = key.T.astype(BF)
            ones_row = jnp.where(lax.broadcasted_iota(jnp.int32, (16, TB), 0) == 0, 1.0, 0.0)
            vat_ref[:, rows] = jnp.concatenate([value.T, ones_row], axis=0).astype(BF)

    project(lo, core, hi)
    project(1 - lo, core, 1 - hi)
    for copy in half_z + [own_pair[1], came_pair[1]] + pair_late:
        copy.wait_recv()
    for low, w in ((1 - lo, hi), (lo, 1 - hi)):
        piece = x_buf.at[:, low, core, w]
        rest.append(net.copy(piece, piece, other_core))
    start_all(rest)
    for copy in share:
        copy.wait_recv()
    project(1 - lo, core, hi)
    project(lo, core, 1 - hi)
    project(lo, 1 - core, hi)
    project(1 - lo, 1 - core, 1 - hi)
    for copy in rest:
        copy.wait_recv()
    store = pltpu.make_async_copy(x_buf, x_seq, local.at[0])
    store.start()
    project(1 - lo, 1 - core, hi)
    project(lo, 1 - core, 1 - hi)
    meta_out[...] = meta_all[...]
    smalls_out[...] = smalls_all[...]

    wait_all(keep)
    for copy in own_y + across_y + cross_late:
        copy.wait_recv()
    later = []
    for m in range(2):
        piece = wholes[m].at[:, unit_rows(m, 3), columns_part(m, lo, 2)]
        later.append(net.copy(piece, piece, pair))
        for d in (1, 3, 2):
            piece = wholes[m].at[:, unit_rows(m, 0), columns_part(m, z, 4)]
            later.append(net.copy(piece, piece, along("z", d)))
    for d in (1, 3, 2):
        for shard, unit, number in ((mine, 2, 1), (across, 1, 2)):
            piece = up_all.at[shard, unit_rows(0, unit, number)]
            later.append(net.copy(piece, piece, along("y", d)))
    piece = out_all.at[:, half_rows(core)]
    later.append(net.copy(piece, piece, other_core))
    for d in range(4):
        piece = down_all.at[(y + d) % 4 * 2 + hi, unit_rows(1, 1, 2)]
        later.append(net.copy(piece, piece, wrap))
    later += qkv_along_y(qkv_all, net, 0, 16)
    start_all(later)

    position = lax.axis_index("seq") * 2 + hi

    def result(b, recv_at):
        there = head_tile(context, position)
        return remote(blocks.at[b], there, back_send.at[b], back_recv.at[recv_at], (y, b // 2, b % 2))

    own_result = pltpu.make_async_copy(blocks.at[position], head_tile(context, position), back_local)

    @pl.loop(0, 4)
    def _(step):
        at = (step + z + 1) % 4
        columns = pl.ds(aligned(at * 1024, 1024), 1024)
        queries = qat_ref[:, columns]
        peak = jnp.full((1, 1024), -jnp.inf, F32)
        total = jnp.zeros((80, 1024), F32)
        for j in range(8):
            keys = slice(j * 512, (j + 1) * 512)
            logits = dot(ka_ref[keys, :], queries)
            new_peak = jnp.maximum(peak, jnp.max(logits, axis=0, keepdims=True))
            expos = jnp.exp(logits - new_peak).astype(BF)
            total = total * jnp.exp(peak - new_peak) + dot(vat_ref[:, keys], expos)
            peak = new_peak
        sums = total[HD : HD + 1]
        found = total[:HD] / sums
        wide_ref[:, columns] = found
        lse_ref[:, columns] = peak + jnp.log(sums)
        low = found.astype(BF)
        for j in range(8):
            b = at * 8 + j
            blocks[b] = low[:, j * TB : (j + 1) * TB]

            @pl.when(b != position)
            def _():
                result(b, position).start()

            @pl.when(b == position)
            def _():
                own_result.start()

    store.wait()
    for copy in [swap] + own_pair + own_z + came_pair + came_z + half_z + pair_late + share + rest:
        copy.wait_send()
    for copy in cross_first + cross_early + cross_late + own_small + across_small + own_y + across_y:
        copy.wait_send()
    wait_all(later)

    @pl.loop(1, NB)
    def _(shift):
        b = (position + shift) % NB
        result(b, b).wait()

    own_result.wait()


def front(tokens, segments, flags, vectors, b_up, w_out, w_up, w_down, w_qkv):
    shape = jax.ShapeDtypeStruct
    in_vmem = pl.BlockSpec(memory_space=pltpu.VMEM)
    return pl.pallas_call(
        front_kernel,
        in_specs=[ANY] + [in_vmem] * 4 + [ANY] * 4,
        out_specs=[ANY] + [in_vmem] * 2 + [ANY] * 4 + [in_vmem] * 5 + [ANY] + [in_vmem] * 2,
        out_shape=[
            shape((4, 2, 2, 2, TB, D), BF),
            shape((NB, 8, TB), jnp.int32),
            shape((8, 16, 128), F32),
            shape((8, 128, D), BF),
            shape((8, 128, 2048), BF),
            shape((8, 256, D), BF),
            shape((8, 128, 3 * D), BF),
            shape((128, L), BF),
            shape((L, 128), BF),
            shape((L, 128), BF),
            shape((HD, L), BF),
            shape((L, HD), BF),
            shape((D, 2 * TB), BF),
            shape((HD, L), F32),
            shape((1, L), F32),
        ],
        scratch_shapes=[
            pltpu.VMEM((80, L), BF),
            pltpu.VMEM((NB, HD, TB), BF),
            pltpu.VMEM((4, 2, 2, 2, TB, D), BF),
            pltpu.VMEM((2, TB, D), BF),
            pltpu.VMEM((128, D), BF),
            pltpu.VMEM((2, 128, 2048), BF),
            pltpu.VMEM((256, D), BF),
            pltpu.VMEM((128, 3 * D), BF),
            pltpu.VMEM((2, 8, TB), jnp.int32),
            pltpu.VMEM((2, 128, 384), BF),
            pltpu.VMEM((16, 128), F32),
            pltpu.VMEM((NB, 8, TB), jnp.int32),
            pltpu.VMEM((8, 128, 384), BF),
            pltpu.VMEM((8, 16, 128), F32),
            pltpu.VMEM((D, 3 * HD), BF),
            pltpu.VMEM((8, 3 * HD), F32),
            pltpu.SemaphoreType.DMA((FRONT_COPIES,)),
            pltpu.SemaphoreType.DMA((FRONT_COPIES,)),
            pltpu.SemaphoreType.DMA((12,)),
            *swap_sems(),
            *swap_sems(),
        ],
        name="front",
        compiler_params=pltpu.CompilerParams(
            collective_id=1, has_side_effects=True, vmem_limit_bytes=VMEM_CAP
        ),
    )(tokens, segments, flags, vectors, b_up, w_out, w_up, w_down, w_qkv)


def qkv_along_y(qkv_all, net, first, count):
    _, y, _, core = place()
    copies = []
    for d in (1, 3, 2):
        for w in range(2):
            piece = qkv_all.at[y * 2 + w, pl.ds(aligned(core * 64 + first, 16), count)]
            copies.append(net.copy(piece, piece, along("y", d)))
    return copies


def turned(first, second):
    return dot(first, second, ((0,), (0,)))


def gelu_both(u):
    rate = 0.7978845608028654
    square = u * u
    curve = jnp.tanh(rate * (u + 0.044715 * (square * u)))
    half = 0.5 * (1.0 + curve)
    slope = half + 0.5 * u * (1.0 - curve * curve) * (rate * (1.0 + 0.134145 * square))
    return u * half, slope


def fold(values):
    return jnp.sum(values.reshape(values.shape[0] // 8, 8, values.shape[1]), axis=0)


ROWS = 256
CHUNK = 32
SMALLS = 16


def middle_kernel(
    context_in, meta, tokens, teacher, flags, smalls, out_all, up_all, down_all, a0,
    states, resid_out, do, g_ref, sums_out, count_out, qkv_all,
    context, context_s, w_out, w_up, w_down, h, act, slope, send_one, come_one, send_two, come_two,
    gb, gu, ga, ga_s, normed, hidden, rate, work, resid, gct, stage, count, counts, valid,
    send, recv, local, back_send, back_recv, back_local,
):
    x, y, z, core = place()
    mine = y * 2 + x // 2
    twin = sibling()
    loads = [
        pltpu.make_async_copy(context_in, context, local.at[6]),
        pltpu.make_async_copy(out_all, w_out, local.at[0]),
        pltpu.make_async_copy(up_all, w_up, local.at[1]),
    ]
    load_down = pltpu.make_async_copy(down_all, w_down, local.at[2])
    start_all(loads + [load_down])
    greet_signal(shard_greet())
    greet_wait(shard_greet())
    net = Transfers(send, recv)
    later = qkv_along_y(qkv_all, net, 16, 48)
    valid_here = jnp.sum(meta[:, 1, :].astype(F32), axis=0, keepdims=True)
    count[...] = jnp.broadcast_to(jnp.sum(valid_here, axis=1, keepdims=True), (8, 128))
    ahead = [net.copy(count, counts.at[mine], target) for target in shard_greet()]
    start_all(ahead + later)
    own_count = pltpu.make_async_copy(count, counts.at[mine], local.at[3])
    own_count.start()
    for s in range(2):
        column = jnp.broadcast_to(flags[s : s + 1, :].astype(F32), (128, 128)).T
        valid[128 * s : 128 * (s + 1), :] = column

    def vector(row):
        return jnp.concatenate([smalls[i, row : row + 1, :] for i in range(8)], axis=1)

    out_bias, gain_one, offset_one, down_bias, gain_two, offset_two = [vector(row) for row in range(2, 8)]
    zeros = jnp.zeros((8, D), F32)
    wait_all(loads)
    give_context = net.copy(context, context_s, twin)
    give_context.start()
    work[...] = turned(context[...], w_out[...].reshape(D, D))

    @pl.loop(0, ROWS // CHUNK)
    def _(i):
        rows = pl.ds(aligned(i * CHUNK, CHUNK), CHUNK)
        total = tokens[rows, :].astype(F32) + work[rows, :] + out_bias
        centre = total - jnp.mean(total, axis=1, keepdims=True)
        scale = lax.rsqrt(jnp.mean(centre * centre, axis=1, keepdims=True) + EPS)
        unit = centre * scale
        normed[rows, :] = unit
        rate[rows, :] = jnp.broadcast_to(scale, (CHUNK, 128))
        full = unit * gain_one + offset_one
        hidden[rows, :] = full
        h[0, rows, :] = full.astype(BF)

    give_hidden = net.copy(h.at[0], h.at[1], twin)
    give_hidden.start()
    for slot in range(2):
        if slot == 1:
            give_hidden.wait()
        for k in range(8):
            columns = slice(256 * k, 256 * (k + 1))
            bias = jnp.concatenate([smalls[k, pl.ds(8 + 2 * core + e, 1), :] for e in range(2)], axis=1)
            u = dot(h[slot], w_up[:, :, columns].reshape(D, 256)) + bias
            value, incline = gelu_both(u)
            act[slot, :, columns] = value.astype(BF)
            slope[slot, :, columns] = incline
    load_down.wait()
    send_one[...] = dot(act[1], w_down[...].reshape(2048, D))
    give_one = net.copy(send_one, come_one, twin)
    give_one.start()
    work[...] = dot(act[0], w_down[...].reshape(2048, D))
    give_one.wait()
    wait_all(ahead)
    own_count.wait()
    total_count = jnp.sum(counts[...], axis=0)
    count_out[...] = total_count
    factor = (128 * ROWS) / total_count[:1, :1]

    def loss_rows(i, carried):
        rows = pl.ds(aligned(i * CHUNK, CHUNK), CHUNK)
        total = hidden[rows, :] + (work[rows, :] + come_one[rows, :] + down_bias)
        centre = total - jnp.mean(total, axis=1, keepdims=True)
        scale = lax.rsqrt(jnp.mean(centre * centre, axis=1, keepdims=True) + EPS)
        unit = centre * scale
        final = unit * gain_two + offset_two
        states[rows, :] = final.astype(BF)
        differ = final - teacher[rows, :].astype(F32)
        held = valid[rows, :1] * differ
        grad = factor * held
        weighted = grad * gain_two
        back = weighted - jnp.mean(weighted, axis=1, keepdims=True)
        back = scale * (back - unit * jnp.mean(weighted * unit, axis=1, keepdims=True))
        resid[rows, :] = back
        low = back.astype(BF)
        gb[0, rows, :] = low
        return (
            carried[0] + fold(grad * unit),
            carried[1] + fold(grad),
            carried[2] + fold(low.astype(F32)),
            carried[3] + fold(held * differ),
        )

    gain_two_sum, offset_two_sum, down_sum, error = lax.fori_loop(
        0, ROWS // CHUNK, loss_rows, (zeros, zeros, zeros, zeros)
    )
    give_branch = net.copy(gb.at[0], gb.at[1], twin)
    give_branch.start()
    up_sums = []
    for slot in range(2):
        if slot == 1:
            give_branch.wait()
        for k in range(8):
            columns = slice(256 * k, 256 * (k + 1))
            pulled = dot(gb[slot], w_down[k], ((1,), (1,))) * slope[slot, :, columns]
            low = pulled.astype(BF)
            gu[slot, :, columns] = low
            up_sums.append(fold(low.astype(F32)))
    for i in range(8):
        send_two[:, 128 * i : 128 * (i + 1)] = dot(gu[1], w_up[i], ((1,), (1,)))
    give_two = net.copy(send_two, come_two, twin)
    give_two.start()
    for i in range(8):
        work[:, 128 * i : 128 * (i + 1)] = dot(gu[0], w_up[i], ((1,), (1,)))
    give_two.wait()

    def first_norm_rows(i, carried):
        rows = pl.ds(aligned(i * CHUNK, CHUNK), CHUNK)
        grad = resid[rows, :] + (work[rows, :] + come_two[rows, :])
        unit = normed[rows, :]
        weighted = grad * gain_one
        back = weighted - jnp.mean(weighted, axis=1, keepdims=True)
        back = rate[rows, :1] * (back - unit * jnp.mean(weighted * unit, axis=1, keepdims=True))
        resid_out[rows, :] = back
        low = back.astype(BF)
        ga[rows, :] = low
        return (carried[0] + fold(grad * unit), carried[1] + fold(grad), carried[2] + fold(low.astype(F32)))

    gain_one_sum, offset_one_sum, out_sum = lax.fori_loop(0, ROWS // CHUNK, first_norm_rows, (zeros, zeros, zeros))
    give_attended = net.copy(ga.at[:, pl.ds(aligned((1 - core) * 512, 512), 512)], ga_s, twin)
    give_attended.start()
    gct[...] = dot(w_out[...].reshape(D, D), ga[...], ((1,), (1,))).astype(BF)
    back_start, back_wait = swap_copies(
        lambda b: head_tile(gct, b), lambda b: do.at[b], (back_send, back_recv, back_local)
    )
    back_start()

    error = jnp.broadcast_to(jnp.sum(jnp.sum(error, axis=0, keepdims=True), axis=1, keepdims=True), (1, 128))
    lines = [out_sum, gain_one_sum, offset_one_sum, down_sum, gain_two_sum, offset_two_sum]
    lines = [jnp.sum(line, axis=0, keepdims=True) for line in lines]
    for i in range(8):
        columns = slice(128 * i, 128 * (i + 1))
        sums_out[i] = jnp.zeros((SMALLS, 128), F32)
        for row, line in enumerate(lines):
            sums_out[i, row : row + 1, :] = line[:, columns]
        both = jnp.sum(up_sums[i] + up_sums[8 + i], axis=0, keepdims=True)
        for e in range(2):
            sums_out[i, pl.ds(6 + 2 * core + e, 1), :] = both[:, 128 * e : 128 * (e + 1)]
        sums_out[i, 10:11, :] = error

    give_context.wait()
    give_attended.wait()

    def stored(i):
        return pltpu.make_async_copy(stage.at[i % 2], g_ref.at[i // 2, i % 2], local.at[4 + i % 2])

    for i in range(8):
        if i >= 2:
            stored(i - 2).wait()
        tall = slice(128 * i, 128 * (i + 1))
        wide = slice(256 * i, 256 * (i + 1))
        up = turned(h[0, :, tall], gu[0]) + turned(h[1, :, tall], gu[1])
        for k in range(4):
            stage[i % 2, 128 * k : 128 * (k + 1), :] = up[:, 512 * k : 512 * (k + 1)].astype(BF)
        down = turned(act[0, :, wide], gb[0]) + turned(act[1, :, wide], gb[1])
        for k in range(2):
            stage[i % 2, 512 + 256 * k : 768 + 256 * k, :] = down[:, 512 * k : 512 * (k + 1)].astype(BF)
        own_half = ga[:, pl.ds(aligned(core * 512, 512), 512)]
        out = dot(context[tall, :], own_half) + dot(context_s[tall, :], ga_s[...])
        stage[i % 2, 1024:, :] = out.astype(BF)
        stored(i).start()
    stored(6).wait()
    stored(7).wait()
    back_wait()
    wait_all(later)


def middle(context, meta, tokens, teacher, flags, smalls, out_all, up_all, down_all, qkv_all):
    shape = jax.ShapeDtypeStruct
    in_vmem = pl.BlockSpec(memory_space=pltpu.VMEM)
    dma = pltpu.SemaphoreType.DMA
    wide = pltpu.VMEM((ROWS, D), F32)
    return pl.pallas_call(
        middle_kernel,
        in_specs=[ANY] + [in_vmem] * 5 + [ANY] * 4,
        out_specs=[in_vmem, in_vmem, ANY, ANY, in_vmem, in_vmem, ANY],
        out_shape=[
            shape((ROWS, D), BF),
            shape((ROWS, D), F32),
            shape((NB, HD, TB), BF),
            shape((4, 2, 1152, 512), BF),
            shape((8, SMALLS, 128), F32),
            shape((8, 128), F32),
            shape(qkv_all.shape, BF),
        ],
        input_output_aliases={9: 6},
        scratch_shapes=[
            pltpu.VMEM((D, ROWS), BF),
            pltpu.VMEM((D, ROWS), BF),
            pltpu.VMEM((8, 128, D), BF),
            pltpu.VMEM((8, 128, 2048), BF),
            pltpu.VMEM((8, 256, D), BF),
            pltpu.VMEM((2, ROWS, D), BF),
            pltpu.VMEM((2, ROWS, 2048), BF),
            pltpu.VMEM((2, ROWS, 2048), F32),
            wide,
            wide,
            wide,
            wide,
            pltpu.VMEM((2, ROWS, D), BF),
            pltpu.VMEM((2, ROWS, 2048), BF),
            pltpu.VMEM((ROWS, D), BF),
            pltpu.VMEM((ROWS, 512), BF),
            wide,
            wide,
            pltpu.VMEM((ROWS, 128), F32),
            wide,
            wide,
            pltpu.VMEM((D, ROWS), BF),
            pltpu.VMEM((2, 1152, 512), BF),
            pltpu.VMEM((8, 128), F32),
            pltpu.VMEM((8, 8, 128), F32),
            pltpu.VMEM((ROWS, 128), F32),
            dma((32,)),
            dma((32,)),
            dma((10,)),
            *swap_sems(),
        ],
        name="middle",
        compiler_params=pltpu.CompilerParams(
            collective_id=3, has_side_effects=True, vmem_limit_bytes=VMEM_CAP
        ),
    )(context, meta, tokens, teacher, flags, smalls, out_all, up_all, down_all, qkv_all)


BACK_KEYS = 256
BACK_STEPS = L // BACK_KEYS
BACK_WIDTH = 1024


def back_prepare(qat, do, wide, lse, queries, grads, grad_rows):
    for j in range(L // BACK_WIDTH):
        columns = slice(j * BACK_WIDTH, (j + 1) * BACK_WIDTH)
        grad_t = jnp.concatenate([do[j * (BACK_WIDTH // TB) + i] for i in range(BACK_WIDTH // TB)], axis=1)
        wider = grad_t.astype(F32)
        delta = jnp.sum(wider * wide[:, columns], axis=0, keepdims=True)
        grads[:HD, columns] = grad_t
        grads[HD:, columns] = jnp.concatenate([three_pieces(-delta), jnp.zeros((61, BACK_WIDTH), BF)], axis=0)
        queries[:96, columns] = qat[:96, columns]
        queries[96:, columns] = jnp.concatenate(
            [three_pieces(-lse[:, columns]), jnp.zeros((29, BACK_WIDTH), BF)], axis=0
        )
        grad_rows[columns, :] = wider.T.astype(BF)


def back_kernel(
    qat, ka, va, kt, q8, do, wide, lse, smalls, x_seq, g_ref, a0,
    projected, heads_out, shard_out, smalls_out, qkv_all,
    x_buf, queries, grads, grad_rows, dq, d_ref, mine_ref, parts_ref, sum_ref, heads_buf, small_buf, small_sum, small_all,
    send, recv, local, dk_send, dk_recv, dk_local, dq_send, dq_recv, dq_local, spread_send, spread_recv, *reduce_refs,
):
    x, y, z, core = place()
    shard_at = y * 2 + x // 2
    seq = lax.axis_index("seq")
    mine = seq * 2 + x // 2
    net = (g_ref,) + reduce_refs

    def shard_device(d):
        other = (shard_at + d) % 8
        return other, (other // 2, seq, other % 2)

    load_x = pltpu.make_async_copy(x_seq, x_buf, local.at[0])
    load_x.start()
    shard_others = [shard_device(d)[1] for d in range(1, 8)]
    greet_signal(shard_others)
    back_prepare(qat, do, wide, lse, queries, grads, grad_rows)
    dq[...] = jnp.zeros_like(dq)
    greet_wait(shard_others)
    for part in range(3):
        reduce_start(part, net)
    far = Transfers(send, recv)
    small_out = [far.copy(smalls.at[shard_device(d)[0]], small_buf.at[shard_at], shard_device(d)[1]) for d in range(1, 8)]
    start_all(small_out)
    small_buf[shard_at] = smalls[shard_at]
    rows = half_rows(core)
    weights = far.copy(qkv_all.at[:, rows], qkv_all.at[:, rows], sibling())
    weights.start()

    def landing(first, count):
        return projected.at[pl.ds(first, count), pl.ds(aligned(seq * HD, HD), HD), pl.ds(aligned((x // 2) * TB, TB), TB)]

    def block_device(b):
        return (y, b // 2, b % 2)

    def dk_copy(b, recv_at):
        return remote(d_ref.at[b, pl.ds(1, 2)], landing(1, 2), dk_send.at[b], dk_recv.at[recv_at], block_device(b))

    def dq_copy(b, recv_at):
        return remote(d_ref.at[b, pl.ds(0, 1)], landing(0, 1), dq_send.at[b], dq_recv.at[recv_at], block_device(b))

    dk_own = pltpu.make_async_copy(d_ref.at[mine, pl.ds(1, 2)], landing(1, 2), dk_local)
    dq_own = pltpu.make_async_copy(d_ref.at[mine, pl.ds(0, 1)], landing(0, 1), dq_local)

    @pl.loop(0, BACK_STEPS)
    def _(step):
        at = (step + 4 * (z + 1)) % BACK_STEPS
        keys = pl.ds(aligned(at * BACK_KEYS, BACK_KEYS), BACK_KEYS)
        ka_part, va_part, kt_part = ka[keys, :], va[keys, :], kt[:, keys]
        dk = jnp.zeros((BACK_KEYS, HD), F32)
        dv = jnp.zeros((BACK_KEYS, HD), F32)
        for j in range(L // BACK_WIDTH):
            columns = slice(j * BACK_WIDTH, (j + 1) * BACK_WIDTH)
            probs = jnp.exp(dot(ka_part, queries[:, columns]))
            raw = (probs * dot(va_part, grads[:, columns])).astype(BF)
            dv = dv + dot(probs.astype(BF), grad_rows[columns, :])
            dk = dk + dot(raw, q8[columns, :])
            dq[:, columns] += dot(kt_part, raw)
        dk_t, dv_t = dk.T.astype(BF), dv.T.astype(BF)
        for i in range(BACK_KEYS // TB):
            b = at * (BACK_KEYS // TB) + i
            d_ref[b, 1] = dk_t[:, i * TB : (i + 1) * TB]
            d_ref[b, 2] = dv_t[:, i * TB : (i + 1) * TB]

            @pl.when(b != mine)
            def _():
                dk_copy(b, mine).start()

            @pl.when(b == mine)
            def _():
                dk_own.start()

        @pl.when(step == 4)
        def _():
            first_relay(net)

        @pl.when(step == 9)
        def _():
            reduce_step(0, 1, net)

        @pl.when(step == 11)
        def _():
            reduce_step(0, 0, net)

        @pl.when(step == 13)
        def _():
            reduce_step(0, 2, net)
            reduce_step(1, 1, net)

    for b in range(NB):
        d_ref[b, 0] = (dq[:, b * TB : (b + 1) * TB] * 0.125).astype(BF)

    @pl.loop(1, NB)
    def _(shift):
        dq_copy((mine + shift) % NB, mine).start()

    dq_own.start()
    steps = [
        spread_steps(part, reduce_refs[6 + part].at[0], (local.at[pl.ds(1, 3)], spread_send, spread_recv), shard_out)
        for part in range(3)
    ]
    reduce_step(2, 1, net)
    steps[1][0]()
    wait_all(small_out)
    small_sum[...] = jnp.sum(small_buf[...], axis=0)

    load_x.wait()
    left = jnp.concatenate([d_ref[b].reshape(3 * HD, TB) for b in range(NB)], axis=1)
    sums = dot(jnp.ones((8, L), BF), left, ((1,), (1,)))
    gap = jnp.zeros((1, 128 - HD), F32)
    tail = jnp.concatenate(
        [
            jnp.concatenate([sums[:1, :HD], gap], axis=1),
            jnp.concatenate([sums[:1, 2 * HD :], gap], axis=1),
            jnp.zeros((14, 128), F32),
        ],
        axis=0,
    ).astype(BF)
    for i in range(4):
        total = dot(left, x_buf[:, :, 256 * i : 256 * (i + 1)].reshape(L, 256))
        for k in range(2):
            mine_ref[2 * i + k, : 3 * HD, :] = total[:, 128 * k : 128 * (k + 1)].astype(BF)
            mine_ref[2 * i + k, 3 * HD :, :] = tail
    part_out = [far.copy(mine_ref.at[shard_device(d)[0]], parts_ref.at[d], shard_device(d)[1]) for d in range(1, 8)]
    start_all(part_out)

    reduce_step(1, 2, net)
    reduce_step(1, 0, net)
    wait_all(part_out)
    added = mine_ref[shard_at].astype(F32)
    for d in range(1, 8):
        added = added + parts_ref[d].astype(F32)
    sum_ref[...] = added.astype(BF)
    heads_buf[seq // 2, core] = sum_ref[...]
    small_all[seq // 2, core] = small_sum[...]
    head_out = []
    for d in range(1, 8):
        target = (y, (seq + 2 * d) % 16, x // 2)
        head_out.append(far.copy(sum_ref, heads_buf.at[seq // 2, core], target))
        head_out.append(far.copy(small_sum, small_all.at[seq // 2, core], target))
    start_all(head_out)
    for part in (2, 0):
        reduce_step(2, part, net)
        steps[part][0]()
    for part in (1, 2, 0):
        steps[part][1]()
    wait_all(head_out)
    across = [
        far.copy(heads_buf.at[:, core], heads_buf.at[:, core], sibling()),
        far.copy(small_all.at[:, core], small_all.at[:, core], sibling()),
    ]
    start_all(across)
    shared = []
    for part in (1, 2, 0):
        steps[part][2]()
        piece = shard_out.at[core, pl.ds(FIRST[part], 8 * PIECE[part])]
        shared.append(far.copy(piece, piece, sibling()))
        shared[-1].start()

    @pl.loop(1, NB)
    def _(shift):
        b = (mine + shift) % NB
        dk_copy(b, b).wait()
        dq_copy(b, b).wait()

    dk_own.wait()
    dq_own.wait()
    weights.wait()
    wait_all(across)
    for i in range(8):
        heads_out[2 * i] = heads_buf[i, 0]
        heads_out[2 * i + 1] = heads_buf[i, 1]
    smalls_out[...] = jnp.sum(small_all[...].reshape(16, 16, 128), axis=0)
    wait_all(shared)


def back(qat, ka, va, kt, q8, do, wide, lse, smalls, x_seq, g, qkv_all):
    shape = jax.ShapeDtypeStruct
    in_vmem = pl.BlockSpec(memory_space=pltpu.VMEM)
    dma = pltpu.SemaphoreType.DMA
    return pl.pallas_call(
        back_kernel,
        in_specs=[in_vmem] * 9 + [ANY] * 3,
        out_specs=[ANY, in_vmem, ANY, in_vmem, ANY],
        out_shape=[
            shape((3, D, 2 * TB), BF),
            shape((H, 208, 128), BF),
            shape((2, 1152, 512), BF),
            shape((16, 128), F32),
            shape(qkv_all.shape, BF),
        ],
        input_output_aliases={11: 4},
        scratch_shapes=[
            pltpu.VMEM((NB, TB, D), BF),
            pltpu.VMEM((128, L), BF),
            pltpu.VMEM((128, L), BF),
            pltpu.VMEM((L, HD), BF),
            pltpu.VMEM((HD, L), F32),
            pltpu.VMEM((NB, 3, HD, TB), BF),
            pltpu.VMEM((8, 208, 128), BF),
            pltpu.VMEM((8, 208, 128), BF),
            pltpu.VMEM((208, 128), BF),
            pltpu.VMEM((8, 2, 208, 128), BF),
            pltpu.VMEM((8, 16, 128), F32),
            pltpu.VMEM((16, 128), F32),
            pltpu.VMEM((8, 2, 16, 128), F32),
            dma((40,)),
            dma((40,)),
            dma((4,)),
            *swap_sems(),
            *swap_sems(),
            dma((3, 8)),
            dma((3, 8)),
            *reduce_scratch(),
        ],
        name="attend_back",
        compiler_params=pltpu.CompilerParams(
            collective_id=4, has_side_effects=True, vmem_limit_bytes=VMEM_CAP
        ),
    )(qat, ka, va, kt, q8, do, wide, lse, smalls, x_seq, g, qkv_all)


def finish_kernel(
    projected, qkv_ref, resid_ref, heads_ref, shard_ref, tokens_ref, grad_qkv, grad_out, grad_up, grad_down
):
    step = pl.program_id(0)
    tokens_ref[...] = resid_ref[...] + dot(projected[...], qkv_ref[...], ((0,), (1,)))
    for c in range(2):
        columns = slice(512 * c, 512 * (c + 1))
        for j in range(2):
            piece = shard_ref[c, pl.ds(aligned(step * 128, 128), 128), 256 * j : 256 * (j + 1)]
            grad_up[:, 512 * j + 256 * c : 512 * j + 256 * (c + 1)] = piece.astype(F32)
        rows = pl.ds(aligned(512 + 256 * c + (step % 2) * 128, 128), 128)
        grad_down[:, columns] = shard_ref[step // 2, rows, :].astype(F32)
        grad_out[:, columns] = shard_ref[c, pl.ds(aligned(1024 + step * 32, 32), 32), :].astype(F32)

    @pl.when(step == 0)
    def _():
        for p in range(3):
            for pair in range(8):
                both = [heads_ref[2 * pair + k, p * HD : (p + 1) * HD, :].astype(F32) for k in range(2)]
                at = p * D + pair * 128
                grad_qkv[:, at : at + 128] = jnp.concatenate(both, axis=0).T


def finish(projected, qkv, resid, heads, shard):
    shape = jax.ShapeDtypeStruct

    def whole(dims):
        return pl.BlockSpec(dims, lambda i: (0,) * len(dims))

    return pl.pallas_call(
        finish_kernel,
        grid=(4,),
        in_specs=[
            whole((3 * D, 2 * TB)),
            pl.BlockSpec((256, 3 * D), lambda i: (i, 0)),
            pl.BlockSpec((2 * TB, 256), lambda i: (0, i)),
            whole((H, 208, 128)),
            whole((2, 1152, 512)),
        ],
        out_specs=[
            pl.BlockSpec((2 * TB, 256), lambda i: (0, i)),
            whole((128, 3 * D)),
            pl.BlockSpec((32, D), lambda i: (i, 0)),
            pl.BlockSpec((128, 1024), lambda i: (0, i)),
            pl.BlockSpec((128, D), lambda i: (i, 0)),
        ],
        out_shape=[
            shape((2 * TB, D), F32),
            shape((128, 3 * D), F32),
            shape((128, D), F32),
            shape((128, FF), F32),
            shape((512, D), F32),
        ],
        name="finish",
        compiler_params=pltpu.CompilerParams(vmem_limit_bytes=VMEM_CAP),
    )(projected, qkv, resid, heads, shard)


def on_device(
    tokens,
    segments,
    valid_flags,
    teacher,
    w_qkv,
    b_query,
    b_value,
    w_out,
    b_out,
    ln1_gain,
    ln1_bias,
    w_up,
    b_up,
    w_down,
    b_down,
    ln2_gain,
    ln2_bias,
):
    seq_local, row_local, _ = tokens.shape
    token_rows = seq_local * row_local
    shard_at = lax.axis_index("dp") * 2 + lax.axis_index("wshard")

    vectors = jnp.stack([b_query, b_value, b_out, ln1_gain, ln1_bias, b_down, ln2_gain, ln2_bias]).astype(F32)
    (
        x_seq, meta_all, smalls_all, out_all, up_all, down_all, qkv_all, qat, ka, va, kt, q8, context, wide, lse
    ) = front(
        tokens, segments, valid_flags, vectors, b_up.reshape(4, 128).astype(F32), w_out, w_up, w_down, w_qkv
    )
    x_seq = x_seq.reshape(NB, TB, D)
    states, grad_resid_one, do, g, small_sums, count, qkv_all = middle(
        context,
        meta_all,
        tokens.reshape(token_rows, D),
        teacher.reshape(token_rows, D),
        valid_flags,
        smalls_all,
        out_all,
        up_all,
        down_all,
        qkv_all,
    )
    projected, heads_out, shard_out, small_out, qkv_all = back(
        qat, ka, va, kt, q8, do, wide, lse, small_sums, x_seq, g, qkv_all
    )
    grad_tokens, grad_qkv, grad_out, grad_up, grad_down = finish(
        projected.reshape(3 * D, token_rows), qkv_all.reshape(D, 3 * D), grad_resid_one, heads_out, shard_out
    )
    own_heads = lax.dynamic_slice(heads_out, (shard_at * 2, 3 * HD, 0), (2, 2, HD)).astype(F32)
    mean_loss = small_out[10, 0] / (D * count[0, 0])
    return (
        states.reshape(seq_local, row_local, D),
        mean_loss,
        grad_tokens.reshape(seq_local, row_local, D),
        grad_qkv,
        own_heads[:, 0].reshape(128),
        own_heads[:, 1].reshape(128),
        grad_out,
        small_out[0],
        small_out[1],
        small_out[2],
        grad_up,
        small_out[6:10].reshape(512),
        grad_down,
        small_out[3],
        small_out[4],
        small_out[5],
    )


def solution(mesh):
    rows = P("dp", ("seq", "wshard"), None)
    flags = P("dp", ("seq", "wshard"))
    matrix = P(("dp", "wshard"), None)
    vector = P(("dp", "wshard"))
    return jax.shard_map(
        on_device,
        mesh=mesh,
        in_specs=(
            rows,
            flags,
            flags,
            rows,
            matrix,
            vector,
            vector,
            matrix,
            vector,
            vector,
            vector,
            matrix,
            vector,
            matrix,
            vector,
            vector,
            vector,
        ),
        out_specs=(
            rows,
            P(),
            rows,
            matrix,
            vector,
            vector,
            matrix,
            vector,
            vector,
            vector,
            matrix,
            vector,
            matrix,
            vector,
            vector,
            vector,
        ),
        check_vma=False,
    )
```

profile of v0, /device:TPU:1, one launch (start us, length us, event | category | flops | bytes accessed | tf_op | source)
XLA Modules:
  0.0 277.7 jit_solution(14673376051903112674)
XLA Ops:
  0.6 0.8 stack.35
  1.4 0.6 convert_element_type.11.vectors
  2.0 1.3 bitcast_convert_fusion.b_up
  3.3 104.4 %front.1 = (bf16[4,2,2,2,128,1024]{5,4,3,2,1,0:T(8,128)(2,1)}, s32[32,8,128]{2,1,0:T(8,128)}, f32[8,16,128]{2,1,0:T(8,128)}, bf16[8,128,1024]{2,1,0:T(8,128)(2,1...) custom-call(bf16[2,128,1024]{2,1,0:T(8,128)(2,1)} %tokens.1, ...), custom_call_target="tpu_custom_call" | custom-call | tf_op jit(solution)/shard_map/front/pallas_call | solution.py:712
  107.7 51.3 %middle.1 = (bf16[256,1024]{1,0:T(8,128)(2,1)}, f32[256,1024]{1,0:T(8,128)}, bf16[32,64,128]{2,1,0:T(8,128)(2,1)}, bf16[4,2,1152,512]{3,2,1,0:T(8,128)(2,1)}, f3...) custom-call(bf16[1024,256]{1,0:T(8,128)(2,1)} %get-tuple-element.48.c, ...), custom_call_target="tpu_custom_call", output_to_operand_aliasing={{6}: (9, {})} | custom-call | tf_op jit(solution)/shard_map/middle/pallas_call | solution.py:986
  159.1 101.0 %attend_back.1 = (bf16[3,1024,256]{2,1,0:T(8,128)(2,1)}, bf16[16,208,128]{2,1,0:T(8,128)(2,1)}, bf16[2,1152,512]{2,1,0:T(8,128)(2,1)}, f32[16,128]{1,0:T(8,128)}, bf16[8,128,3072]{2,1,0:T(8,128)(2,1)}) custom-call(bf16[128,4096]{1,0:T(8,128)(2,1)} %get-tuple-element.56.qat, ...), custom_call_target="tpu_custom_call", output_to_operand_aliasing={{4}: (11, {})} | custom-call | tf_op jit(solution)/shard_map/attend_back/pallas_call | solution.py:1243
  260.0 0.0 copy-start.1
  260.0 0.0 copy-start
  260.0 9.5 %finish.1 = (f32[256,1024]{1,0:T(8,128)}, f32[128,3072]{1,0:T(8,128)}, f32[128,1024]{1,0:T(8,128)}, f32[128,4096]{1,0:T(8,128)}, f32[512,1024]{1,0:T(8,128)}) custom-call(bf16[3072,256]{1,0:T(8,128)(2,1)} %bitcast.36, bf16[1024,3072]{1,0:T(8,128)(2,1)} %bitcast.33, f32[256,1024]{1,0:T(8,128)} %get-tuple-element.72.resid_ref, ...), custom_call_target="tpu_custom_call" | custom-call | tf_op jit(solution)/shard_map/finish/pallas_call | solution.py:1314
  269.6 0.7 dynamic-slice_convert_fusion
  270.3 0.6 reshape_squeeze.6
  270.9 0.6 reshape_squeeze.7
  271.4 0.0 copy-done.1
  271.4 0.5 slice_bitcast_fusion.1
  272.0 0.5 slice.33
  272.5 1.2 slice.34
  275.0 0.6 slice_bitcast_fusion
  275.6 0.0 copy-done
  275.6 0.8 copy.38
  (1 shorter events, 0.0 us)
Async XLA Ops:
  260.0 11.4 %copy-start.1 = (f32[16,128]{1,0:T(8,128)S(1)}, f32[16,128]{1,0:T(8,128)}, u32[]{:S(2)}) copy-start(f32[16,128]{1,0:T(8,128)} %get-tuple-element.68) | copy-start | bytes 24580
  260.0 15.5 %copy-start = (bf16[256,1024]{1,0:T(8,128)(2,1)S(1)}, bf16[256,1024]{1,0:T(8,128)(2,1)}, u32[]{:S(2)}) copy-start(bf16[256,1024]{1,0:T(8,128)(2,1)} %get-tuple-element.55) | copy-start | bytes 1572868
where the time goes:
time: 281 us; the launch traced here: 278 us
  Pallas kernels  266 us (95%)
  local copies, waits for them, and re-layouts  5.62 us (2%)
  between operations  3.32 us (1%)
    pallas_call x1, Pallas kernels, front(): pl.pallas_call(front_kernel, in_specs=[ANY] + [in_vmem] * 4 + [ANY] * 4,...  104 us
    pallas_call x1, Pallas kernels, back(): pl.pallas_call(back_kernel, in_specs=[in_vmem] * 9 + [ANY] * 3, out_specs...  101 us
    pallas_call x1, Pallas kernels, middle(): pl.pallas_call(middle_kernel, in_specs=[ANY] + [in_vmem] * 5 + [ANY] * 4,...  51.3 us
    pallas_call x1, Pallas kernels, finish(): pl.pallas_call(finish_kernel, grid=(4,), in_specs=[whole((3 * D, 2 * TB))...  9.52 us

commit v1 on v0

--- a/solution.py
+++ b/solution.py
@@ -505,17 +505,15 @@
             keep.append(pltpu.make_async_copy(shards[m].at[rows, columns], piece, local.at[1 + 3 * m + k]))
     start_all(keep)
 
-    def along_y(shard, source, out_source, up_unit):
+    def along_y(shard, source, out_source, inner):
         copies = []
         for d in (1, 3, 2):
             there = along("y", d)
             copies.append(net.copy(out_source.at[rows_out], out_all.at[shard, rows_out], there))
             for m in range(2):
                 parts = [(0, columns_part(m, z, 4)), (3, columns_part(m, lo, 2))]
-                if up_unit:
-                    parts.append((1, slice(None)))
-                for unit, columns in parts:
-                    rows = unit_rows(m, unit, 2 if m == 1 and unit == 1 else 1)
+                for unit, columns in parts + ([(1, slice(None))] if inner else []):
+                    rows = unit_rows(m, unit, 2 if unit == 1 else 1)
                     copies.append(net.copy(source(m).at[rows, columns], wholes[m].at[shard, rows, columns], there))
         return copies
 
@@ -574,6 +572,10 @@
         piece = x_buf.at[:, low, core, w]
         share.append(net.copy(piece, piece, other_core))
     start_all(share)
+    cross_late[0].wait_recv()
+    rows = unit_rows(0, 1, 2)
+    across_up = [net.copy(up_all.at[across, rows], up_all.at[across, rows], along("y", d)) for d in (1, 3, 2)]
+    start_all(across_up)
 
     for copy in own_small + across_small:
         copy.wait_recv()
@@ -631,7 +633,7 @@
     smalls_out[...] = smalls_all[...]
 
     wait_all(keep)
-    for copy in own_y + across_y + cross_late:
+    for copy in own_y + across_y + cross_late[1:]:
         copy.wait_recv()
     later = []
     for m in range(2):
@@ -640,16 +642,11 @@
         for d in (1, 3, 2):
             piece = wholes[m].at[:, unit_rows(m, 0), columns_part(m, z, 4)]
             later.append(net.copy(piece, piece, along("z", d)))
-    for d in (1, 3, 2):
-        for shard, unit, number in ((mine, 2, 1), (across, 1, 2)):
-            piece = up_all.at[shard, unit_rows(0, unit, number)]
-            later.append(net.copy(piece, piece, along("y", d)))
     piece = out_all.at[:, half_rows(core)]
     later.append(net.copy(piece, piece, other_core))
     for d in range(4):
         piece = down_all.at[(y + d) % 4 * 2 + hi, unit_rows(1, 1, 2)]
         later.append(net.copy(piece, piece, wrap))
-    later += qkv_along_y(qkv_all, net, 0, 16)
     start_all(later)
 
     position = lax.axis_index("seq") * 2 + hi
@@ -696,6 +693,7 @@
         copy.wait_send()
     for copy in cross_first + cross_early + cross_late + own_small + across_small + own_y + across_y:
         copy.wait_send()
+    wait_all(across_up)
     wait_all(later)
 
     @pl.loop(1, NB)
@@ -760,12 +758,12 @@
     )(tokens, segments, flags, vectors, b_up, w_out, w_up, w_down, w_qkv)
 
 
-def qkv_along_y(qkv_all, net, first, count):
+def qkv_along_y(qkv_all, net):
     _, y, _, core = place()
     copies = []
     for d in (1, 3, 2):
         for w in range(2):
-            piece = qkv_all.at[y * 2 + w, pl.ds(aligned(core * 64 + first, 16), count)]
+            piece = qkv_all.at[y * 2 + w, half_rows(core)]
             copies.append(net.copy(piece, piece, along("y", d)))
     return copies
 
@@ -812,7 +810,7 @@
     greet_signal(shard_greet())
     greet_wait(shard_greet())
     net = Transfers(send, recv)
-    later = qkv_along_y(qkv_all, net, 16, 48)
+    later = qkv_along_y(qkv_all, net)
     valid_here = jnp.sum(meta[:, 1, :].astype(F32), axis=0, keepdims=True)
     count[...] = jnp.broadcast_to(jnp.sum(valid_here, axis=1, keepdims=True), (8, 128))
     ahead = [net.copy(count, counts.at[mine], target) for target in shard_greet()]
@@ -1149,22 +1147,16 @@
             reduce_step(0, 2, net)
             reduce_step(1, 1, net)
 
-    for b in range(NB):
-        d_ref[b, 0] = (dq[:, b * TB : (b + 1) * TB] * 0.125).astype(BF)
-
-    @pl.loop(1, NB)
-    def _(shift):
-        dq_copy((mine + shift) % NB, mine).start()
-
-    dq_own.start()
+    reduce_step(1, 0, net)
+    reduce_step(1, 2, net)
     steps = [
         spread_steps(part, reduce_refs[6 + part].at[0], (local.at[pl.ds(1, 3)], spread_send, spread_recv), shard_out)
         for part in range(3)
     ]
     reduce_step(2, 1, net)
     steps[1][0]()
-    wait_all(small_out)
-    small_sum[...] = jnp.sum(small_buf[...], axis=0)
+    for b in range(NB):
+        d_ref[b, 0] = (dq[:, b * TB : (b + 1) * TB] * 0.125).astype(BF)
 
     load_x.wait()
     left = jnp.concatenate([d_ref[b].reshape(3 * HD, TB) for b in range(NB)], axis=1)
@@ -1186,8 +1178,16 @@
     part_out = [far.copy(mine_ref.at[shard_device(d)[0]], parts_ref.at[d], shard_device(d)[1]) for d in range(1, 8)]
     start_all(part_out)
 
-    reduce_step(1, 2, net)
-    reduce_step(1, 0, net)
+    @pl.loop(1, NB)
+    def _(shift):
+        dq_copy((mine + shift) % NB, mine).start()
+
+    dq_own.start()
+    for part in (2, 0):
+        reduce_step(2, part, net)
+        steps[part][0]()
+    wait_all(small_out)
+    small_sum[...] = jnp.sum(small_buf[...], axis=0)
     wait_all(part_out)
     added = mine_ref[shard_at].astype(F32)
     for d in range(1, 8):
@@ -1201,9 +1201,6 @@
         head_out.append(far.copy(sum_ref, heads_buf.at[seq // 2, core], target))
         head_out.append(far.copy(small_sum, small_all.at[seq // 2, core], target))
     start_all(head_out)
-    for part in (2, 0):
-        reduce_step(2, part, net)
-        steps[part][0]()
     for part in (1, 2, 0):
         steps[part][1]()
     wait_all(head_out)

time: 281 us -> 286 us (1.018)
  Pallas kernels: 266 us -> 271 us
    pallas_call x1, Pallas kernels: 104 us -> 110 us  [front(): pl.pallas_call(front_kernel, in_specs=[ANY] + [in_vmem] * 4 + [ANY] * 4,...]
where the time goes in v1:
time: 286 us; the launch traced here: 283 us
  Pallas kernels  271 us (95%)
  local copies, waits for them, and re-layouts  5.62 us (2%)
  between operations  3.32 us (1%)
    pallas_call x1, Pallas kernels, front(): pl.pallas_call(front_kernel, in_specs=[ANY] + [in_vmem] * 4 + [ANY] * 4,...  110 us
    pallas_call x1, Pallas kernels, back(): pl.pallas_call(back_kernel, in_specs=[in_vmem] * 9 + [ANY] * 3, out_specs...  100 us
    pallas_call x1, Pallas kernels, middle(): pl.pallas_call(middle_kernel, in_specs=[ANY] + [in_vmem] * 5 + [ANY] * 4,...  51.4 us
    pallas_call x1, Pallas kernels, finish(): pl.pallas_call(finish_kernel, grid=(4,), in_specs=[whole((3 * D, 2 * TB))...  9.51 us

profile of v1, /device:TPU:1, one launch (start us, length us, event | category | flops | bytes accessed | tf_op | source)
XLA Modules:
  0.0 282.6 jit_solution(12971018446844315165)
XLA Ops:
  0.6 0.8 stack.35
  1.4 0.6 convert_element_type.11.vectors
  2.0 1.3 bitcast_convert_fusion.b_up
  3.3 109.9 %front.1 = (bf16[4,2,2,2,128,1024]{5,4,3,2,1,0:T(8,128)(2,1)}, s32[32,8,128]{2,1,0:T(8,128)}, f32[8,16,128]{2,1,0:T(8,128)}, bf16[8,128,1024]{2,1,0:T(8,128)(2,1...) custom-call(bf16[2,128,1024]{2,1,0:T(8,128)(2,1)} %tokens.1, ...), custom_call_target="tpu_custom_call" | custom-call | tf_op jit(solution)/shard_map/front/pallas_call | solution.py:710
  113.2 51.4 %middle.1 = (bf16[256,1024]{1,0:T(8,128)(2,1)}, f32[256,1024]{1,0:T(8,128)}, bf16[32,64,128]{2,1,0:T(8,128)(2,1)}, bf16[4,2,1152,512]{3,2,1,0:T(8,128)(2,1)}, f3...) custom-call(bf16[1024,256]{1,0:T(8,128)(2,1)} %get-tuple-element.48.c, ...), custom_call_target="tpu_custom_call", output_to_operand_aliasing={{6}: (9, {})} | custom-call | tf_op jit(solution)/shard_map/middle/pallas_call | solution.py:984
  164.7 100.3 %attend_back.1 = (bf16[3,1024,256]{2,1,0:T(8,128)(2,1)}, bf16[16,208,128]{2,1,0:T(8,128)(2,1)}, bf16[2,1152,512]{2,1,0:T(8,128)(2,1)}, f32[16,128]{1,0:T(8,128)}, bf16[8,128,3072]{2,1,0:T(8,128)(2,1)}) custom-call(bf16[128,4096]{1,0:T(8,128)(2,1)} %get-tuple-element.56.qat, ...), custom_call_target="tpu_custom_call", output_to_operand_aliasing={{4}: (11, {})} | custom-call | tf_op jit(solution)/shard_map/attend_back/pallas_call | solution.py:1240
  265.0 0.0 copy-start.1
  265.0 0.0 copy-start
  265.0 9.5 %finish.1 = (f32[256,1024]{1,0:T(8,128)}, f32[128,3072]{1,0:T(8,128)}, f32[128,1024]{1,0:T(8,128)}, f32[128,4096]{1,0:T(8,128)}, f32[512,1024]{1,0:T(8,128)}) custom-call(bf16[3072,256]{1,0:T(8,128)(2,1)} %bitcast.36, bf16[1024,3072]{1,0:T(8,128)(2,1)} %bitcast.33, f32[256,1024]{1,0:T(8,128)} %get-tuple-element.72.resid_ref, ...), custom_call_target="tpu_custom_call" | custom-call | tf_op jit(solution)/shard_map/finish/pallas_call | solution.py:1311
  274.5 0.7 dynamic-slice_convert_fusion
  275.2 0.6 reshape_squeeze.6
  275.8 0.6 reshape_squeeze.7
  276.4 0.0 copy-done.1
  276.4 0.5 slice_bitcast_fusion.1
  276.9 0.5 slice.33
  277.4 1.2 slice.34
  279.9 0.6 slice_bitcast_fusion
  280.5 0.0 copy-done
  280.5 0.8 copy.38
  (1 shorter events, 0.0 us)
Async XLA Ops:
  265.0 11.4 %copy-start.1 = (f32[16,128]{1,0:T(8,128)S(1)}, f32[16,128]{1,0:T(8,128)}, u32[]{:S(2)}) copy-start(f32[16,128]{1,0:T(8,128)} %get-tuple-element.68) | copy-start | bytes 24580
  265.0 15.5 %copy-start = (bf16[256,1024]{1,0:T(8,128)(2,1)S(1)}, bf16[256,1024]{1,0:T(8,128)(2,1)}, u32[]{:S(2)}) copy-start(bf16[256,1024]{1,0:T(8,128)(2,1)} %get-tuple-element.55) | copy-start | bytes 1572868
